TPU v7x, 256 devices: a whole 4x4x8 slice. The times are simulated.
256 devices in a mesh: depth: 256 (over y, x, z, core).
Axes of the slice: x: 4, y: 4, z: 8, core: 2. Of those that a mesh axis runs over, the one named last changes fastest.
Arguments:
- weights: bfloat16 [256, 1024, 1024], P('depth'), may hold values from -0.1875 to 0.1875
- gains: float32 [256, 1024], P('depth'), may hold values from 0.1 to 1.9
- states: float32 [256, 512, 1024], P('depth'), may hold values from -1200 to 1200
- adjoints: float32 [256, 512, 1024], P('depth'), may hold values from -0.26516503 to 0.26516503
Outputs:
- grad_weight: bfloat16 [256, 1024, 1024], P('depth')
- grad_gain: float32 [256, 1024], P('depth')
All inputs are finite; a program needn't handle non-finite values.
Results may differ from a plain program's by a relative error of at most 0.006.
Values sent between devices are 32-bit elements; how exact they have to be, the bound alone decides.
A program may use at most 64 MiB of HBM per device.

v0:
```python
import jax
import jax.numpy as jnp
from jax import lax

SWEEPS = 4


eps = 1e-06


def layer_terms(state, adjoint, gains, weights):
    inverse = lax.rsqrt(jnp.mean(state * state, axis=-1, keepdims=True) + eps)
    normed = state * inverse
    scaled = (normed * gains[:, None, :]).astype(jnp.bfloat16)
    preact = jnp.einsum("ltd,lde->lte", scaled.astype(jnp.float32), weights.astype(jnp.float32))
    squash = jax.nn.sigmoid(preact)
    output = state + preact * squash
    pre_grad = (adjoint * squash * (1.0 + preact * (1.0 - squash))).astype(jnp.bfloat16)
    feat_grad = jnp.einsum(
        "lte,lde->ltd", pre_grad.astype(jnp.float32), weights.astype(jnp.float32)
    )
    gained = feat_grad * gains[:, None, :]
    carried = adjoint + inverse * (
        gained - normed * jnp.mean(gained * normed, axis=-1, keepdims=True)
    )
    return (output, carried, scaled, pre_grad, normed, feat_grad)


def reference(weights, gains, states, adjoints):
    state, adjoint = (states, adjoints)
    for sweep_index in range(SWEEPS):
        output, carried, scaled, pre_grad, normed, feat_grad = layer_terms(
            state, adjoint, gains, weights
        )
        state = jnp.concatenate([state[:1], output[:-1]], axis=0)
        adjoint = jnp.concatenate([carried[1:], adjoint[-1:]], axis=0)
    output, carried, scaled, pre_grad, normed, feat_grad = layer_terms(
        state, adjoint, gains, weights
    )
    grad_weight = jnp.einsum(
        "ltd,lte->lde", scaled.astype(jnp.float32), pre_grad.astype(jnp.float32)
    ).astype(jnp.bfloat16)
    grad_gain = jnp.sum(normed * feat_grad, axis=1)
    return (grad_weight, grad_gain)


def solution(mesh):
    return reference
```

profile of v0, /device:TPU:24, one launch (start us, length us, event | category | flops | bytes accessed | tf_op | source)
XLA Modules:
  0.0 166.0 jit_solution(9608874759581449783)
XLA Ops:
  0.6 0.0 copy-start
  0.6 0.0 copy-start.1
  0.7 2.2 %collective-permute-start.5 = (f32[1,512,1024]{2,1,0:T(8,128)}, f32[1,512,1024]{2,1,0:T(8,128)}, u32[]{:S(2)}, u32[]{:S(2)}) collective-permute-start(f32[1,512,1024]{2,1,0:T(8,128)} %param.3), channel_id=6, source_target_pairs={{255,0}} | collective-permute-start | bytes 6291464 | tf_op args[3]
  2.8 1.8 %multiply_reduce_fusion.8 = f32[512]{0:T(512)S(1)} fusion(f32[1,512,1024]{2,1,0:T(8,128)} %param), kind=kLoop, calls=%fused_computation.99 | loop fusion | flops 1048064 | bytes 2099200 | tf_op jit(solution)/reduce_sum | solution.py:12
  4.7 0.0 copy-start.3
  4.7 1.3 fusion.53
  6.0 0.3 copy-done.3
  6.3 2.0 %multiply_reduce_fusion.3 = (f32[512]{0:T(512)S(1)}, f32[512,1024]{1,0:T(8,128)S(1)}) fusion(f32[1,512,1024]{2,1,0:T(8,128)S(1)} %copy-done.1, f32[512]{0:T(512)S(1)} %add_rsqrt_fusion.4, f32[1024]{0:T(1024)S(1)} %bitcast.231, bf16[1,1024,1024]{2,1,0:T(8,128)(2,1)S(1)} %copy-done, f32[1,512,1024]{2,1,0:T(8,128)S(1)} %copy-done.3, f32[512,1024]{1,0:T(8,128)S(1)} %fusion.53), kind=kOutput, calls=%fused_computation.85 | convolution fusion | flops 1080557056 | bytes 10493952 | tf_op jit(solution)/lte,lde->ltd/dot_general | solution.py:19
  8.2 0.0 copy-start.5
  8.2 2.9 %multiply_add_fusion.3 = (f32[1,512,1024]{2,1,0:T(8,128)}, f32[1,512,1024]{2,1,0:T(8,128)}) fusion(f32[1,512,1024]{2,1,0:T(8,128)S(1)} %copy-done.3, f32[512,1024]{1,0:T(8,128)S(1)} %get-tuple-element.17, f32[1,512,1024]{2,1,0:T(8,128)S(1)} %copy-done.1, f32[512]{0:T(512)S(1)} %add_rsqrt_fusion.4, f32[512]{0:T(512)S(1)} %broadcast_multiply_fusion.3, ...), kind=kLoop, calls=%fused_computation.84 | loop fusion | flops 5767168 | bytes 12591104 | tf_op jit(solution)/add | solution.py:23
  11.2 1.9 %collective-permute-start = (f32[1,512,1024]{2,1,0:T(8,128)}, f32[1,512,1024]{2,1,0:T(8,128)}, u32[]{:S(2)}, u32[]{:S(2)}) collective-permute-start(f32[1,512,1024]{2,1,0:T(8,128)} %get-tuple-element.15), channel_id=1, source_target_pairs={{0,1},{1,2},{2,3},{3,4},{4,5},{5,6},{6,7},{7,8},{8,9},{9,10},{10,1... | collective-permute-start | bytes 6291464 | tf_op jit(solution)/slice | solution.py:35
  13.1 9.6 %collective-permute-start.4 = (f32[1,512,1024]{2,1,0:T(8,128)}, f32[1,512,1024]{2,1,0:T(8,128)}, u32[]{:S(2)}, u32[]{:S(2)}) collective-permute-start(f32[1,512,1024]{2,1,0:T(8,128)} %get-tuple-element.14), channel_id=5, source_target_pairs={{1,0},{2,1},{3,2},{4,3},{5,4},{6,5},{7,6},{8,7},{9,8},{10,9},{11,1... | collective-permute-start | bytes 6291464 | tf_op jit(solution)/add | solution.py:23
  22.7 0.0 collective-permute-done.5
  22.7 2.0 %collective-permute-start.6 = (f32[1,512,1024]{2,1,0:T(8,128)}, f32[1,512,1024]{2,1,0:T(8,128)}, u32[]{:S(2)}, u32[]{:S(2)}) collective-permute-start(f32[1,512,1024]{2,1,0:T(8,128)} %collective-permute-done.5), channel_id=7, source_target_pairs={{0,255}} | collective-permute-start | bytes 6291464 | tf_op jit(solution)/slice | solution.py:36
  24.6 0.6 dynamic-slice.16
  25.9 18.9 %collective-permute-done = f32[1,512,1024]{2,1,0:T(8,128)} collective-permute-done((f32[1,512,1024]{2,1,0:T(8,128)}, f32[1,512,1024]{2,1,0:T(8,128)}, u32[]{:S(2)}, u32[]{:S(2)}) %collective-permute-start) | collective-permute-done | bytes 2097184 | tf_op jit(solution)/slice | solution.py:35
  44.8 2.0 %multiply_reduce_fusion.7 = (f32[512]{0:T(512)S(1)}, f32[1,512,1024]{2,1,0:T(8,128)S(1)}) fusion(f32[1,512,1024]{2,1,0:T(8,128)} %collective-permute-done, pred[]{:T(512)S(6)} %compare.13, f32[1,512,1024]{2,1,0:T(8,128)} %param, pred[]{:T(512)S(6)} %compare.12), kind=kLoop, calls=%fused_computation.96 | loop fusion | flops 2620928 | bytes 6293506 | tf_op jit(solution)/reduce_sum | solution.py:12
  46.8 1.3 fusion.51
  48.1 0.0 collective-permute-done.4
  48.1 0.0 collective-permute-done.6
  48.1 3.4 %multiply_reduce_fusion.2 = (f32[512]{0:T(512)S(1)}, f32[512,1024]{1,0:T(8,128)S(1)}) fusion(f32[1,512,1024]{2,1,0:T(8,128)S(1)} %get-tuple-element.7, f32[512]{0:T(512)S(1)} %add_rsqrt_fusion.3, f32[1024]{0:T(1024)S(1)} %bitcast.234, bf16[1,1024,1024]{2,1,0:T(8,128)(2,1)S(1)} %copy-done, f32[512,1024]{1,0:T(8,128)S(1)} %fusion.51, ...), kind=kOutput, calls=%fused_computation.82 | convolution fusion | flops 1082129920 | bytes 12591106 | tf_op jit(solution)/lte,lde->ltd/dot_general | solution.py:19
  51.5 0.0 copy-start.2
  51.5 2.9 %multiply_add_fusion.2 = (f32[1,512,1024]{2,1,0:T(8,128)S(1)}, f32[1,512,1024]{2,1,0:T(8,128)S(1)}) fusion(f32[512,1024]{1,0:T(8,128)S(1)} %get-tuple-element.19, f32[1,512,1024]{2,1,0:T(8,128)S(1)} %get-tuple-element.7, f32[512]{0:T(512)S(1)} %add_rsqrt_fusion.3, f32[512]{0:T(512)S(1)} %broadcast_multiply_fusion.2, f32[1024]{0:T(1024)S(1)} %bitcast.235, ...), kind=kLoop, calls=%fused_computation.81 | loop fusion | flops 7340032 | bytes 14688258 | tf_op jit(solution)/add | solution.py:23
  54.4 1.9 %collective-permute-start.1 = (f32[1,512,1024]{2,1,0:T(8,128)S(1)}, f32[1,512,1024]{2,1,0:T(8,128)S(1)}, u32[]{:S(2)}, u32[]{:S(2)}) collective-permute-start(f32[1,512,1024]{2,1,0:T(8,128)S(1)} %get-tuple-element.13), channel_id=2, source_target_pairs={{0,1},{1,2},{2,3},{3,4},{4,5},{5,6},{6,7},{7,8},{8,9},{9,10},{10,1... | collective-permute-start | bytes 6291464 | tf_op jit(solution)/slice | solution.py:35
  56.3 8.0 %collective-permute-start.7 = (f32[1,512,1024]{2,1,0:T(8,128)S(1)}, f32[1,512,1024]{2,1,0:T(8,128)S(1)}, u32[]{:S(2)}, u32[]{:S(2)}) collective-permute-start(f32[1,512,1024]{2,1,0:T(8,128)S(1)} %get-tuple-element.12), channel_id=8, source_target_pairs={{1,0},{2,1},{3,2},{4,3},{5,4},{6,5},{7,6},{8,7},{9,8},{10,9},{11,1... | collective-permute-start | bytes 6291464 | tf_op jit(solution)/add | solution.py:23
  64.3 21.6 %collective-permute-done.1 = f32[1,512,1024]{2,1,0:T(8,128)S(1)} collective-permute-done((f32[1,512,1024]{2,1,0:T(8,128)S(1)}, f32[1,512,1024]{2,1,0:T(8,128)S(1)}, u32[]{:S(2)}, u32[]{:S(2)}) %collective-permute-start.1) | collective-permute-done | bytes 2097184 | tf_op jit(solution)/slice | solution.py:35
  85.9 0.5 multiply_reduce_fusion.6
  86.5 1.3 fusion.49
  87.8 0.0 collective-permute-done.7
  87.8 1.8 %multiply_reduce_fusion.1 = (f32[512]{0:T(512)S(1)}, f32[512,1024]{1,0:T(8,128)S(1)}) fusion(f32[1,512,1024]{2,1,0:T(8,128)S(1)} %get-tuple-element.5, f32[512]{0:T(512)S(1)} %add_rsqrt_fusion.2, f32[1024]{0:T(1024)S(1)} %bitcast.237, bf16[1,1024,1024]{2,1,0:T(8,128)(2,1)S(1)} %copy-done, f32[512,1024]{1,0:T(8,128)S(1)} %fusion.49, ...), kind=kOutput, calls=%fused_computation.79 | convolution fusion | flops 1082129920 | bytes 12591106 | tf_op jit(solution)/lte,lde->ltd/dot_general | solution.py:19
  89.6 1.1 multiply_add_fusion.1
  90.7 1.9 %collective-permute-start.2 = (f32[1,512,1024]{2,1,0:T(8,128)S(1)}, f32[1,512,1024]{2,1,0:T(8,128)S(1)}, u32[]{:S(2)}, u32[]{:S(2)}) collective-permute-start(f32[1,512,1024]{2,1,0:T(8,128)S(1)} %get-tuple-element.11), channel_id=3, source_target_pairs={{0,1},{1,2},{2,3},{3,4},{4,5},{5,6},{6,7},{7,8},{8,9},{9,10},{10,1... | collective-permute-start | bytes 6291464 | tf_op jit(solution)/slice | solution.py:35
  92.6 7.9 %collective-permute-start.8 = (f32[1,512,1024]{2,1,0:T(8,128)S(1)}, f32[1,512,1024]{2,1,0:T(8,128)S(1)}, u32[]{:S(2)}, u32[]{:S(2)}) collective-permute-start(f32[1,512,1024]{2,1,0:T(8,128)S(1)} %get-tuple-element.10), channel_id=9, source_target_pairs={{1,0},{2,1},{3,2},{4,3},{5,4},{6,5},{7,6},{8,7},{9,8},{10,9},{11,1... | collective-permute-start | bytes 6291464 | tf_op jit(solution)/add | solution.py:23
  100.6 21.8 %collective-permute-done.2 = f32[1,512,1024]{2,1,0:T(8,128)S(1)} collective-permute-done((f32[1,512,1024]{2,1,0:T(8,128)S(1)}, f32[1,512,1024]{2,1,0:T(8,128)S(1)}, u32[]{:S(2)}, u32[]{:S(2)}) %collective-permute-start.2) | collective-permute-done | bytes 2097184 | tf_op jit(solution)/slice | solution.py:35
  122.3 0.4 multiply_reduce_fusion.5
  122.8 1.3 fusion.47
  124.1 0.0 collective-permute-done.8
  124.1 1.8 %multiply_reduce_fusion = (f32[512]{0:T(512)S(1)}, f32[512,1024]{1,0:T(8,128)S(1)}) fusion(f32[1,512,1024]{2,1,0:T(8,128)S(1)} %get-tuple-element.3, f32[512]{0:T(512)S(1)} %add_rsqrt_fusion.1, f32[1024]{0:T(1024)S(1)} %bitcast.240, bf16[1,1024,1024]{2,1,0:T(8,128)(2,1)S(1)} %copy-done, f32[512,1024]{1,0:T(8,128)S(1)} %fusion.47, ...), kind=kOutput, calls=%fused_computation.76 | convolution fusion | flops 1082129920 | bytes 12591106 | tf_op jit(solution)/lte,lde->ltd/dot_general | solution.py:19
  125.9 1.1 multiply_add_fusion
  127.0 1.9 %collective-permute-start.3 = (f32[1,512,1024]{2,1,0:T(8,128)S(1)}, f32[1,512,1024]{2,1,0:T(8,128)S(1)}, u32[]{:S(2)}, u32[]{:S(2)}) collective-permute-start(f32[1,512,1024]{2,1,0:T(8,128)S(1)} %get-tuple-element.9), channel_id=4, source_target_pairs={{0,1},{1,2},{2,3},{3,4},{4,5},{5,6},{6,7},{7,8},{8,9},{9,10},{10,1... | collective-permute-start | bytes 6291464 | tf_op jit(solution)/slice | solution.py:35
  128.9 8.2 %collective-permute-start.9 = (f32[1,512,1024]{2,1,0:T(8,128)S(1)}, f32[1,512,1024]{2,1,0:T(8,128)S(1)}, u32[]{:S(2)}, u32[]{:S(2)}) collective-permute-start(f32[1,512,1024]{2,1,0:T(8,128)S(1)} %get-tuple-element.8), channel_id=10, source_target_pairs={{1,0},{2,1},{3,2},{4,3},{5,4},{6,5},{7,6},{8,7},{9,8},{10,9},{11,1... | collective-permute-start | bytes 6291464 | tf_op jit(solution)/add | solution.py:23
  137.2 21.6 %collective-permute-done.3 = f32[1,512,1024]{2,1,0:T(8,128)S(1)} collective-permute-done((f32[1,512,1024]{2,1,0:T(8,128)S(1)}, f32[1,512,1024]{2,1,0:T(8,128)S(1)}, u32[]{:S(2)}, u32[]{:S(2)}) %collective-permute-start.3) | collective-permute-done | bytes 2097184 | tf_op jit(solution)/slice | solution.py:35
  158.7 0.4 multiply_reduce_fusion.4
  159.2 1.3 fusion.37
  160.5 0.0 collective-permute-done.9
  160.5 0.9 fusion.6
  161.4 1.9 %fusion = f32[1024]{0:T(1024)} fusion(f32[1,512,1024]{2,1,0:T(8,128)S(1)} %get-tuple-element.1, bf16[1,1024,1024]{2,1,0:T(8,128)(2,1)S(1)} %copy-done, bf16[1,512,1024]{2,1,0:T(8,128)(2,1)S(1)} %fusion.6, f32[512]{0:T(512)S(1)} %add_rsqrt_fusion), kind=kOutput, calls=%fused_computation.1 | convolution fusion | flops 1075313664 | bytes 5249024 | tf_op jit(solution)/lte,lde->ltd/dot_general | solution.py:19
  163.3 2.7 %convert_bitcast_fusion = bf16[1,1024,1024]{2,1,0:T(8,128)(2,1)} fusion(bf16[1,512,1024]{2,1,0:T(8,128)(2,1)S(1)} %fusion.6, f32[1,512,1024]{2,1,0:T(8,128)S(1)} %get-tuple-element.1, f32[512]{0:T(512)S(1)} %add_rsqrt_fusion, f32[1024]{0:T(1024)S(1)} %bitcast.243), kind=kOutput, calls=%fused_computation.74 | convolution fusion | flops 1076363264 | bytes 5249024 | tf_op jit(solution)/ltd,lte->lde/dot_general | solution.py:40
  (15 shorter events, 0.1 us)
Async XLA Ops:
  0.6 4.0 %copy-start = (bf16[1,1024,1024]{2,1,0:T(8,128)(2,1)S(1)}, bf16[1,1024,1024]{2,1,0:T(8,128)(2,1)}, u32[]{:S(2)}) copy-start(bf16[1,1024,1024]{2,1,0:T(8,128)(2,1)} %param.2) | copy-start | bytes 6291460
  0.6 4.0 %copy-start.1 = (f32[1,512,1024]{2,1,0:T(8,128)S(1)}, f32[1,512,1024]{2,1,0:T(8,128)}, u32[]{:S(2)}) copy-start(f32[1,512,1024]{2,1,0:T(8,128)} %param) | copy-start | bytes 6291460
  0.7 4.0 %copy-start.4 = (f32[1,1024]{1,0:T(1,128)S(1)}, f32[1,1024]{1,0:T(1,128)}, u32[]{:S(2)}) copy-start(f32[1,1024]{1,0:T(1,128)} %param.1) | copy-start | bytes 12292
  0.7 22.0 %collective-permute-start.5 = (f32[1,512,1024]{2,1,0:T(8,128)}, f32[1,512,1024]{2,1,0:T(8,128)}, u32[]{:S(2)}, u32[]{:S(2)}) collective-permute-start(f32[1,512,1024]{2,1,0:T(8,128)} %param.3), channel_id=6, source_target_pairs={{255,0}} | collective-permute-start | bytes 6291464 | tf_op args[3]
  4.7 1.6 copy-start.3
  8.2 16.4 %copy-start.5 = (s32[256]{0:T(256)S(1)}, s32[256]{0:T(256)}, u32[]{:S(2)}) copy-start(s32[256]{0:T(256)} %constant.116) | copy-start | bytes 3076
  11.2 33.6 %collective-permute-start = (f32[1,512,1024]{2,1,0:T(8,128)}, f32[1,512,1024]{2,1,0:T(8,128)}, u32[]{:S(2)}, u32[]{:S(2)}) collective-permute-start(f32[1,512,1024]{2,1,0:T(8,128)} %get-tuple-element.15), channel_id=1, source_target_pairs={{0,1},{1,2},{2,3},{3,4},{4,5},{5,6},{6,7},{7,8},{8,9},{9,10},{10,1... | collective-permute-start | bytes 6291464 | tf_op jit(solution)/slice | solution.py:35
  13.1 35.0 %collective-permute-start.4 = (f32[1,512,1024]{2,1,0:T(8,128)}, f32[1,512,1024]{2,1,0:T(8,128)}, u32[]{:S(2)}, u32[]{:S(2)}) collective-permute-start(f32[1,512,1024]{2,1,0:T(8,128)} %get-tuple-element.14), channel_id=5, source_target_pairs={{1,0},{2,1},{3,2},{4,3},{5,4},{6,5},{7,6},{8,7},{9,8},{10,9},{11,1... | collective-permute-start | bytes 6291464 | tf_op jit(solution)/add | solution.py:23
  22.7 25.4 %collective-permute-start.6 = (f32[1,512,1024]{2,1,0:T(8,128)}, f32[1,512,1024]{2,1,0:T(8,128)}, u32[]{:S(2)}, u32[]{:S(2)}) collective-permute-start(f32[1,512,1024]{2,1,0:T(8,128)} %collective-permute-done.5), channel_id=7, source_target_pairs={{0,255}} | collective-permute-start | bytes 6291464 | tf_op jit(solution)/slice | solution.py:36
  51.5 34.4 %copy-start.2 = (f32[1,512,1024]{2,1,0:T(8,128)S(1)}, f32[1,512,1024]{2,1,0:T(8,128)}, u32[]{:S(2)}) copy-start(f32[1,512,1024]{2,1,0:T(8,128)} %param) | copy-start | bytes 6291460
  54.4 31.6 %collective-permute-start.1 = (f32[1,512,1024]{2,1,0:T(8,128)S(1)}, f32[1,512,1024]{2,1,0:T(8,128)S(1)}, u32[]{:S(2)}, u32[]{:S(2)}) collective-permute-start(f32[1,512,1024]{2,1,0:T(8,128)S(1)} %get-tuple-element.13), channel_id=2, source_target_pairs={{0,1},{1,2},{2,3},{3,4},{4,5},{5,6},{6,7},{7,8},{8,9},{9,10},{10,1... | collective-permute-start | bytes 6291464 | tf_op jit(solution)/slice | solution.py:35
  56.3 31.5 %collective-permute-start.7 = (f32[1,512,1024]{2,1,0:T(8,128)S(1)}, f32[1,512,1024]{2,1,0:T(8,128)S(1)}, u32[]{:S(2)}, u32[]{:S(2)}) collective-permute-start(f32[1,512,1024]{2,1,0:T(8,128)S(1)} %get-tuple-element.12), channel_id=8, source_target_pairs={{1,0},{2,1},{3,2},{4,3},{5,4},{6,5},{7,6},{8,7},{9,8},{10,9},{11,1... | collective-permute-start | bytes 6291464 | tf_op jit(solution)/add | solution.py:23
  90.7 31.6 %collective-permute-start.2 = (f32[1,512,1024]{2,1,0:T(8,128)S(1)}, f32[1,512,1024]{2,1,0:T(8,128)S(1)}, u32[]{:S(2)}, u32[]{:S(2)}) collective-permute-start(f32[1,512,1024]{2,1,0:T(8,128)S(1)} %get-tuple-element.11), channel_id=3, source_target_pairs={{0,1},{1,2},{2,3},{3,4},{4,5},{5,6},{6,7},{7,8},{8,9},{9,10},{10,1... | collective-permute-start | bytes 6291464 | tf_op jit(solution)/slice | solution.py:35
  92.6 31.5 %collective-permute-start.8 = (f32[1,512,1024]{2,1,0:T(8,128)S(1)}, f32[1,512,1024]{2,1,0:T(8,128)S(1)}, u32[]{:S(2)}, u32[]{:S(2)}) collective-permute-start(f32[1,512,1024]{2,1,0:T(8,128)S(1)} %get-tuple-element.10), channel_id=9, source_target_pairs={{1,0},{2,1},{3,2},{4,3},{5,4},{6,5},{7,6},{8,7},{9,8},{10,9},{11,1... | collective-permute-start | bytes 6291464 | tf_op jit(solution)/add | solution.py:23
  127.0 31.7 %collective-permute-start.3 = (f32[1,512,1024]{2,1,0:T(8,128)S(1)}, f32[1,512,1024]{2,1,0:T(8,128)S(1)}, u32[]{:S(2)}, u32[]{:S(2)}) collective-permute-start(f32[1,512,1024]{2,1,0:T(8,128)S(1)} %get-tuple-element.9), channel_id=4, source_target_pairs={{0,1},{1,2},{2,3},{3,4},{4,5},{5,6},{6,7},{7,8},{8,9},{9,10},{10,1... | collective-permute-start | bytes 6291464 | tf_op jit(solution)/slice | solution.py:35
  128.9 31.6 %collective-permute-start.9 = (f32[1,512,1024]{2,1,0:T(8,128)S(1)}, f32[1,512,1024]{2,1,0:T(8,128)S(1)}, u32[]{:S(2)}, u32[]{:S(2)}) collective-permute-start(f32[1,512,1024]{2,1,0:T(8,128)S(1)} %get-tuple-element.8), channel_id=10, source_target_pairs={{1,0},{2,1},{3,2},{4,3},{5,4},{6,5},{7,6},{8,7},{9,8},{10,9},{11,1... | collective-permute-start | bytes 6291464 | tf_op jit(solution)/add | solution.py:23
where the time goes:
time: 167 us; the launch traced here: 166 us
  waiting for transfers between devices  83.8 us (50%)
  starting transfers between devices  45.6 us (27%)
  matrix products  20 us (12%)
  other arithmetic  14.1 us (8%)
    slice x4, waiting for transfers between devices, reference(): state = jnp.concatenate([state[:1], output[:-1]], axis=0)  83.8 us
    add x4, starting transfers between devices, layer_terms(): adjoint + inverse * (gained - normed * jnp.mean(gained * normed, axis=-1,...  33.8 us
    dot_general x5, matrix products, layer_terms(): jnp.einsum('lte,lde->ltd', pre_grad.astype(jnp.float32), weights.astype(j...  10.8 us
    add x4, other arithmetic, layer_terms(): adjoint + inverse * (gained - normed * jnp.mean(gained * normed, axis=-1,...  8.01 us
    slice x4, starting transfers between devices, reference(): state = jnp.concatenate([state[:1], output[:-1]], axis=0)  7.67 us
    dot_general x5, matrix products, layer_terms(): jnp.einsum('ltd,lde->lte', scaled.astype(jnp.float32), weights.astype(jnp...  6.52 us
    reduce_sum x5, other arithmetic, layer_terms(): inverse = lax.rsqrt(jnp.mean(state * state, axis=-1, keepdims=True) + eps)  5.16 us
  transfers between devices with their start and end apart: 10, of which 4 were waited for; matrix products, arithmetic and copies ran while one was open for 10% of the time, Pallas kernels for 0%

commit v1 on v0

v1 whole, which is shorter than its diff:
```python
import functools

import jax
import jax.numpy as jnp
from jax import lax
from jax.experimental import pallas as pl
from jax.experimental.pallas import tpu as pltpu
from jax.sharding import PartitionSpec as P

SWEEPS = 4
EPS = 1e-06
MESH = pl.DeviceIdType.MESH
CHUNKS = (64, 64, 128, 128, 64, 64)
TILE = 256


def kernel(
    n,
    weights_ref,
    gains_ref,
    states_ref,
    adjoints_ref,
    grad_weight_ref,
    grad_gain_ref,
    weights,
    gains,
    state,
    adjoint,
    state_out,
    adjoint_out,
    normed,
    slope,
    product,
    scaled,
    pre_grad,
    total,
    gain_total,
    result,
    load_sem,
    state_sem,
    adjoint_sem,
    state_send_sem,
    adjoint_send_sem,
    result_sem,
):
    me = lax.axis_index("depth")
    right, left = lax.rem(me + 1, n), lax.rem(me + n - 1, n)
    width = weights.shape[0]
    tiles = width // TILE
    starts = [sum(CHUNKS[:c]) for c in range(len(CHUNKS))]
    chunks = list(enumerate(zip(starts, CHUNKS)))

    barrier = pltpu.get_barrier_semaphore()
    for neighbour in (left, right):
        pl.semaphore_signal(barrier, inc=1, device_id=(neighbour,), device_id_type=MESH)

    def load_state(sweep, c):
        rows = pl.ds(starts[c], CHUNKS[c])
        return pltpu.make_async_copy(
            states_ref.at[0, rows], state.at[sweep, rows], state_sem.at[sweep, c]
        )

    def load_adjoint(sweep, c):
        rows = pl.ds(starts[c], CHUNKS[c])
        return pltpu.make_async_copy(
            adjoints_ref.at[0, rows], adjoint.at[sweep, rows], adjoint_sem.at[sweep, c]
        )

    def send_state(sweep, c):
        rows = pl.ds(starts[c], CHUNKS[c])
        slot = lax.rem(sweep, 2)
        return pltpu.make_async_remote_copy(
            src_ref=state_out.at[slot, rows],
            dst_ref=state.at[sweep + 1, rows],
            send_sem=state_send_sem.at[slot, c],
            recv_sem=state_sem.at[sweep + 1, c],
            device_id=(right,),
            device_id_type=MESH,
        )

    def send_adjoint(sweep, c):
        rows = pl.ds(starts[c], CHUNKS[c])
        slot = lax.rem(sweep, 2)
        return pltpu.make_async_remote_copy(
            src_ref=adjoint_out.at[slot, rows],
            dst_ref=adjoint.at[sweep + 1, rows],
            send_sem=adjoint_send_sem.at[slot, c],
            recv_sem=adjoint_sem.at[sweep + 1, c],
            device_id=(left,),
            device_id_type=MESH,
        )

    load_gains = pltpu.make_async_copy(gains_ref, gains, load_sem.at[0])
    load_gains.start()
    load_state(0, 0).start()
    load_weights = pltpu.make_async_copy(weights_ref.at[0], weights, load_sem.at[1])
    load_weights.start()
    for c, _ in chunks:
        if c:
            load_state(0, c).start()
        load_adjoint(0, c).start()

    @pl.when(me == 0)
    def _():
        for sweep in range(1, SWEEPS + 1):
            for c, _ in chunks:
                load_state(sweep, c).start()

    @pl.when(me == n - 1)
    def _():
        for sweep in range(1, SWEEPS + 1):
            for c, _ in chunks:
                load_adjoint(sweep, c).start()

    def forward(sweep, c, first, last):
        start, count = starts[c], CHUNKS[c]
        rows = pl.ds(start, count)
        load_state(sweep, c).wait()
        if first and c == 0:
            load_gains.wait()
        block = state[sweep, rows, :]
        inverse = lax.rsqrt(jnp.mean(block * block, axis=-1, keepdims=True) + EPS)
        unit = block * inverse
        normed[pl.ds(0, count), :] = unit
        scaled[rows, :] = (unit * gains[...]).astype(jnp.bfloat16)
        if first and c == 0:
            load_weights.wait()
        slot = lax.rem(sweep, 2)
        for t in range(tiles):
            columns = pl.ds(t * TILE, TILE)
            preact = jnp.dot(
                scaled[rows, :], weights[:, columns], preferred_element_type=jnp.float32
            )
            squash = 0.5 * jnp.tanh(0.5 * preact) + 0.5
            slope[pl.ds(0, count), columns] = squash * (1.0 + preact * (1.0 - squash))
            if not last:
                state_out[slot, rows, columns] = state[sweep, rows, columns] + preact * squash
        return inverse

    def backward(sweep, c, inverse, last):
        start, count = starts[c], CHUNKS[c]
        rows = pl.ds(start, count)
        here = pl.ds(0, count)
        load_adjoint(sweep, c).wait()
        pre_grad[rows, :] = (adjoint[sweep, rows, :] * slope[here, :]).astype(jnp.bfloat16)
        slot = lax.rem(sweep, 2)
        projection = jnp.zeros((count, 1), jnp.float32)
        for t in range(tiles):
            columns = pl.ds(t * TILE, TILE)
            feat_grad = lax.dot_general(
                pre_grad[rows, :],
                weights[columns, :],
                (((1,), (1,)), ((), ())),
                preferred_element_type=jnp.float32,
            )
            if last:
                part = jnp.sum(normed[here, columns] * feat_grad, axis=0, keepdims=True)
                gain_total[:, columns] = part if c == 0 else gain_total[:, columns] + part
            else:
                gained = feat_grad * gains[:, columns]
                product[here, columns] = gained
                projection += jnp.sum(gained * normed[here, columns], axis=-1, keepdims=True)
        if not last:
            projection = projection / width
            adjoint_out[slot, rows, :] = adjoint[sweep, rows, :] + inverse * (
                product[here, :] - normed[here, :] * projection
            )

    def sweep_chunk(sweep, c, first):
        if not isinstance(sweep, int) or sweep >= 2:

            @pl.when(jnp.logical_and(sweep >= 2, me < n - 1))
            def _():
                send_state(sweep - 2, c).wait_send()

            @pl.when(jnp.logical_and(sweep >= 2, me > 0))
            def _():
                send_adjoint(sweep - 2, c).wait_send()

        inverse = forward(sweep, c, first, False)
        if first and c == 0:
            pl.semaphore_wait(barrier, 2)

        @pl.when(me < n - 1)
        def _():
            send_state(sweep, c).start()

        backward(sweep, c, inverse, False)

        @pl.when(me > 0)
        def _():
            send_adjoint(sweep, c).start()

    for c, _ in chunks:
        sweep_chunk(0, c, True)

    @pl.loop(1, SWEEPS)
    def _(sweep):
        for c, _ in chunks:
            sweep_chunk(sweep, c, False)

    def store_result(t):
        columns = pl.ds(t * TILE, TILE)
        return pltpu.make_async_copy(
            result.at[columns], grad_weight_ref.at[0, columns], result_sem.at[t]
        )

    for c, (start, count) in chunks:
        rows = pl.ds(start, count)
        inverse = forward(SWEEPS, c, False, True)
        backward(SWEEPS, c, inverse, True)
        for t in range(tiles):
            columns = pl.ds(t * TILE, TILE)
            part = lax.dot_general(
                scaled[rows, columns],
                pre_grad[rows, :],
                (((0,), (0,)), ((), ())),
                preferred_element_type=jnp.float32,
            )
            if c == 0:
                total[columns, :] = part
            elif c < len(CHUNKS) - 1:
                total[columns, :] += part
            else:
                result[columns, :] = (total[columns, :] + part).astype(jnp.bfloat16)
                store_result(t).start()
    grad_gain_ref[...] = gain_total[...]

    for sweep in range(SWEEPS - 2, SWEEPS):
        for c, _ in chunks:

            @pl.when(me < n - 1)
            def _():
                send_state(sweep, c).wait_send()

            @pl.when(me > 0)
            def _():
                send_adjoint(sweep, c).wait_send()

    for t in range(tiles):
        store_result(t).wait()


def solution(mesh):
    n = mesh.shape["depth"]

    def step(weights, gains, states, adjoints):
        _, tokens, width = states.shape
        assert sum(CHUNKS) == tokens
        largest = max(CHUNKS)
        slots = pltpu.VMEM((SWEEPS + 1, tokens, width), jnp.float32)
        sent = pltpu.VMEM((2, tokens, width), jnp.float32)
        piece = pltpu.VMEM((largest, width), jnp.float32)
        whole = pltpu.VMEM((tokens, width), jnp.bfloat16)
        any_space = pl.BlockSpec(memory_space=pl.ANY)
        return pl.pallas_call(
            functools.partial(kernel, n),
            out_shape=(
                jax.ShapeDtypeStruct((1, width, width), jnp.bfloat16),
                jax.ShapeDtypeStruct((1, width), jnp.float32),
            ),
            in_specs=[any_space] * 4,
            out_specs=(any_space, pl.BlockSpec(memory_space=pltpu.VMEM)),
            scratch_shapes=[
                pltpu.VMEM((width, width), jnp.bfloat16),
                pltpu.VMEM((1, width), jnp.float32),
                slots,
                slots,
                sent,
                sent,
                piece,
                piece,
                piece,
                whole,
                whole,
                pltpu.VMEM((width, width), jnp.float32),
                pltpu.VMEM((1, width), jnp.float32),
                pltpu.VMEM((width, width), jnp.bfloat16),
                pltpu.SemaphoreType.DMA((2,)),
                pltpu.SemaphoreType.DMA((SWEEPS + 1, len(CHUNKS))),
                pltpu.SemaphoreType.DMA((SWEEPS + 1, len(CHUNKS))),
                pltpu.SemaphoreType.DMA((2, len(CHUNKS))),
                pltpu.SemaphoreType.DMA((2, len(CHUNKS))),
                pltpu.SemaphoreType.DMA((width // TILE,)),
            ],
            compiler_params=pltpu.CompilerParams(
                collective_id=0, has_side_effects=True, vmem_limit_bytes=56 * 2**20
            ),
            cost_estimate=pl.CostEstimate(
                flops=2 * tokens * width * width * (2 * SWEEPS + 3),
                bytes_accessed=4 * width * width + 8 * tokens * width,
                transcendentals=tokens * width * (SWEEPS + 1),
            ),
        )(weights, gains, states, adjoints)

    spec = P("depth", None, None)
    return jax.shard_map(
        step,
        mesh=mesh,
        in_specs=(spec, P("depth", None), spec, spec),
        out_specs=(spec, P("depth", None)),
        check_vma=False,
    )
```

time: 167 us -> 111 us (0.66)
  Pallas kernels: 0 us -> 107 us
  waiting for transfers between devices: 83.8 us -> 0 us
  starting transfers between devices: 45.6 us -> 0 us
  matrix products: 20 us -> 0 us
  other arithmetic: 14.1 us -> 0 us
  local copies, waits for them, and re-layouts: 0.89 us -> 3.68 us
    pallas_call x0 -> x1, Pallas kernels: none -> 107 us  [step(): pl.pallas_call(functools.partial(kernel, n), out_shape=(jax.ShapeDtypeStr...]
    slice x5 -> x0, waiting for transfers between devices: 83.8 us -> none  [the longest x4 83.8 us: reference(): state = jnp.concatenate([state[:1], output[:-1]], axis=0)]
    add x4 -> x0, starting transfers between devices: 33.8 us -> none  [layer_terms(): adjoint + inverse * (gained - normed * jnp.mean(gained * normed, axis=-1,...]
    dot_general x11 -> x0, matrix products: 20 us -> none  [the longest x5 10.8 us: layer_terms(): jnp.einsum('lte,lde->ltd', pre_grad.astype(jnp.float32), weights.astype(j...]
    slice x5 -> x0, starting transfers between devices: 9.63 us -> none  [the longest x4 7.67 us: reference(): state = jnp.concatenate([state[:1], output[:-1]], axis=0)]
    add x4 -> x0, other arithmetic: 8.01 us -> none  [layer_terms(): adjoint + inverse * (gained - normed * jnp.mean(gained * normed, axis=-1,...]
    reduce_sum x5 -> x0, other arithmetic: 5.16 us -> none  [layer_terms(): inverse = lax.rsqrt(jnp.mean(state * state, axis=-1, keepdims=True) + eps)]
    unnamed x12 -> x4, local copies, waits for them, and re-layouts: 0.3 us -> 3.68 us
  transfers between devices with their start and end apart: 10 -> 0, of which waited for: 4 -> 0; matrix products, arithmetic and copies ran while one was open for 10% -> 0% of each run, Pallas kernels for 0% -> 0%
where the time goes in v1:
time: 111 us
  Pallas kernels  107 us (96%)
  local copies, waits for them, and re-layouts  3.68 us (3%)
    pallas_call x1, Pallas kernels, step(): pl.pallas_call(functools.partial(kernel, n), out_shape=(jax.ShapeDtypeStr...  107 us
    unnamed x4, local copies, waits for them, and re-layouts  3.68 us

profile of v1, /device:TPU:24, one launch (start us, length us, event | category | flops | bytes accessed | tf_op | source)
XLA Modules:
  0.0 110.9 jit_solution(6941165263755505329)
XLA Ops:
  0.6 106.6 %shard_map.59 = (bf16[1,1024,1024]{2,1,0:T(8,128)(2,1)}, f32[1,1024]{1,0:T(1,128)}) custom-call(bf16[1,1024,1024]{2,1,0:T(8,128)(2,1)} %weights_ref.1, f32[1,1024]{1,0:T(1,128)} %gains_ref.1, f32[1,512,1024]{2,1,0:T(8,128)} %states_ref.1, f32[1,512,1024]{2,1,0:T(8,128)} %adjoints_ref.1), custom_call_target="tpu_custom_call" | custom-call | flops 11811160064 | bytes 8388608 | tf_op jit(solution)/shard_map/pallas_call | solution.py:256
  107.2 0.0 copy-start
  107.2 3.1 %copy.8 = bf16[1,1024,1024]{2,1,0:T(8,128)(2,1)} copy(bf16[1,1024,1024]{2,1,0:T(8,128)(2,1)} %get-tuple-element.4) | data formatting | bytes 4194304
  110.3 0.0 copy-done
  110.3 0.6 copy.9
Async XLA Ops:
  107.2 3.1 %copy-start = (f32[1,1024]{1,0:T(1,128)S(1)}, f32[1,1024]{1,0:T(1,128)}, u32[]{:S(2)}) copy-start(f32[1,1024]{1,0:T(1,128)} %get-tuple-element.5) | copy-start | bytes 12292

commit v2 on v1

--- a/solution.py
+++ b/solution.py
@@ -10,7 +10,9 @@
 SWEEPS = 4
 EPS = 1e-06
 MESH = pl.DeviceIdType.MESH
-CHUNKS = (64, 64, 128, 128, 64, 64)
+CHUNKS = (64, 128, 128, 128, 64)
+TAIL = 64
+STORE = 128
 TILE = 256
 
 
@@ -20,8 +22,10 @@
     gains_ref,
     states_ref,
     adjoints_ref,
-    grad_weight_ref,
-    grad_gain_ref,
+    total,
+    scaled_tail,
+    pre_grad_tail,
+    gain_total,
     weights,
     gains,
     state,
@@ -33,19 +37,16 @@
     product,
     scaled,
     pre_grad,
-    total,
-    gain_total,
-    result,
     load_sem,
     state_sem,
     adjoint_sem,
     state_send_sem,
     adjoint_send_sem,
-    result_sem,
 ):
     me = lax.axis_index("depth")
     right, left = lax.rem(me + 1, n), lax.rem(me + n - 1, n)
     width = weights.shape[0]
+    tokens = state.shape[1]
     tiles = width // TILE
     starts = [sum(CHUNKS[:c]) for c in range(len(CHUNKS))]
     chunks = list(enumerate(zip(starts, CHUNKS)))
@@ -90,27 +91,35 @@
             device_id_type=MESH,
         )
 
+    def load_weights(t):
+        rows = pl.ds(t * TILE, TILE)
+        return pltpu.make_async_copy(
+            weights_ref.at[0, rows], weights.at[rows], load_sem.at[1 + t]
+        )
+
     load_gains = pltpu.make_async_copy(gains_ref, gains, load_sem.at[0])
     load_gains.start()
     load_state(0, 0).start()
-    load_weights = pltpu.make_async_copy(weights_ref.at[0], weights, load_sem.at[1])
-    load_weights.start()
-    for c, _ in chunks:
-        if c:
+    for t in range(tiles):
+        load_weights(t).start()
+    load_adjoint(0, 0).start()
+
+    def load_the_rest():
+        for c, _ in chunks[1:]:
             load_state(0, c).start()
-        load_adjoint(0, c).start()
-
-    @pl.when(me == 0)
-    def _():
-        for sweep in range(1, SWEEPS + 1):
-            for c, _ in chunks:
-                load_state(sweep, c).start()
-
-    @pl.when(me == n - 1)
-    def _():
-        for sweep in range(1, SWEEPS + 1):
-            for c, _ in chunks:
-                load_adjoint(sweep, c).start()
+            load_adjoint(0, c).start()
+
+        @pl.when(me == 0)
+        def _():
+            for sweep in range(1, SWEEPS + 1):
+                for c, _ in chunks:
+                    load_state(sweep, c).start()
+
+        @pl.when(me == n - 1)
+        def _():
+            for sweep in range(1, SWEEPS + 1):
+                for c, _ in chunks:
+                    load_adjoint(sweep, c).start()
 
     def forward(sweep, c, first, last):
         start, count = starts[c], CHUNKS[c]
@@ -124,7 +133,9 @@
         normed[pl.ds(0, count), :] = unit
         scaled[rows, :] = (unit * gains[...]).astype(jnp.bfloat16)
         if first and c == 0:
-            load_weights.wait()
+            for t in range(tiles):
+                load_weights(t).wait()
+            load_the_rest()
         slot = lax.rem(sweep, 2)
         for t in range(tiles):
             columns = pl.ds(t * TILE, TILE)
@@ -199,32 +210,24 @@
         for c, _ in chunks:
             sweep_chunk(sweep, c, False)
 
-    def store_result(t):
-        columns = pl.ds(t * TILE, TILE)
-        return pltpu.make_async_copy(
-            result.at[columns], grad_weight_ref.at[0, columns], result_sem.at[t]
-        )
-
     for c, (start, count) in chunks:
         rows = pl.ds(start, count)
         inverse = forward(SWEEPS, c, False, True)
         backward(SWEEPS, c, inverse, True)
-        for t in range(tiles):
-            columns = pl.ds(t * TILE, TILE)
-            part = lax.dot_general(
-                scaled[rows, columns],
-                pre_grad[rows, :],
-                (((0,), (0,)), ((), ())),
-                preferred_element_type=jnp.float32,
-            )
-            if c == 0:
-                total[columns, :] = part
-            elif c < len(CHUNKS) - 1:
-                total[columns, :] += part
-            else:
-                result[columns, :] = (total[columns, :] + part).astype(jnp.bfloat16)
-                store_result(t).start()
-    grad_gain_ref[...] = gain_total[...]
+        if start >= tokens - TAIL:
+            here = pl.ds(start - (tokens - TAIL), count)
+            scaled_tail[here, :] = scaled[rows, :]
+            pre_grad_tail[here, :] = pre_grad[rows, :]
+        else:
+            for t in range(tiles):
+                columns = pl.ds(t * TILE, TILE)
+                part = lax.dot_general(
+                    scaled[rows, columns],
+                    pre_grad[rows, :],
+                    (((0,), (0,)), ((), ())),
+                    preferred_element_type=jnp.float32,
+                )
+                total[columns, :] = part if c == 0 else total[columns, :] + part
 
     for sweep in range(SWEEPS - 2, SWEEPS):
         for c, _ in chunks:
@@ -237,8 +240,38 @@
             def _():
                 send_adjoint(sweep, c).wait_send()
 
-    for t in range(tiles):
-        store_result(t).wait()
+
+def finish(
+    total,
+    scaled_tail,
+    pre_grad_tail,
+    gain_total,
+    grad_weight_ref,
+    grad_gain_ref,
+    result,
+    result_sem,
+    gain_sem,
+):
+    store_gain = pltpu.make_async_copy(gain_total, grad_gain_ref, gain_sem)
+    store_gain.start()
+    stores = []
+    for t in range(total.shape[0] // STORE):
+        columns = pl.ds(t * STORE, STORE)
+        part = lax.dot_general(
+            scaled_tail[:, columns],
+            pre_grad_tail[...],
+            (((0,), (0,)), ((), ())),
+            preferred_element_type=jnp.float32,
+        )
+        result[columns, :] = (total[columns, :] + part).astype(jnp.bfloat16)
+        store = pltpu.make_async_copy(
+            result.at[columns], grad_weight_ref.at[0, columns], result_sem.at[t]
+        )
+        store.start()
+        stores.append(store)
+    for store in stores:
+        store.wait()
+    store_gain.wait()
 
 
 def solution(mesh):
@@ -253,14 +286,17 @@
         piece = pltpu.VMEM((largest, width), jnp.float32)
         whole = pltpu.VMEM((tokens, width), jnp.bfloat16)
         any_space = pl.BlockSpec(memory_space=pl.ANY)
-        return pl.pallas_call(
+        vmem = pl.BlockSpec(memory_space=pltpu.VMEM)
+        parts = pl.pallas_call(
             functools.partial(kernel, n),
             out_shape=(
-                jax.ShapeDtypeStruct((1, width, width), jnp.bfloat16),
-                jax.ShapeDtypeStruct((1, width), jnp.float32),
-            ),
-            in_specs=[any_space] * 4,
-            out_specs=(any_space, pl.BlockSpec(memory_space=pltpu.VMEM)),
+                pltpu.VMEM((width, width), jnp.float32),
+                pltpu.VMEM((TAIL, width), jnp.bfloat16),
+                pltpu.VMEM((TAIL, width), jnp.bfloat16),
+                pltpu.VMEM((1, width), jnp.float32),
+            ),
+            in_specs=[pl.BlockSpec(memory_space=pltpu.HBM)] * 4,
+            out_specs=(vmem,) * 4,
             scratch_shapes=[
                 pltpu.VMEM((width, width), jnp.bfloat16),
                 pltpu.VMEM((1, width), jnp.float32),
@@ -273,25 +309,41 @@
                 piece,
                 whole,
                 whole,
-                pltpu.VMEM((width, width), jnp.float32),
-                pltpu.VMEM((1, width), jnp.float32),
-                pltpu.VMEM((width, width), jnp.bfloat16),
-                pltpu.SemaphoreType.DMA((2,)),
+                pltpu.SemaphoreType.DMA((1 + width // TILE,)),
                 pltpu.SemaphoreType.DMA((SWEEPS + 1, len(CHUNKS))),
                 pltpu.SemaphoreType.DMA((SWEEPS + 1, len(CHUNKS))),
                 pltpu.SemaphoreType.DMA((2, len(CHUNKS))),
                 pltpu.SemaphoreType.DMA((2, len(CHUNKS))),
-                pltpu.SemaphoreType.DMA((width // TILE,)),
             ],
             compiler_params=pltpu.CompilerParams(
-                collective_id=0, has_side_effects=True, vmem_limit_bytes=56 * 2**20
+                collective_id=0, has_side_effects=True, vmem_limit_bytes=48 * 2**20
             ),
             cost_estimate=pl.CostEstimate(
                 flops=2 * tokens * width * width * (2 * SWEEPS + 3),
                 bytes_accessed=4 * width * width + 8 * tokens * width,
                 transcendentals=tokens * width * (SWEEPS + 1),
             ),
-        )(weights, gains, states, adjoints)
+        )(*(pltpu.with_memory_space_constraint(x, pltpu.HBM) for x in (weights, gains, states, adjoints)))
+        return pl.pallas_call(
+            finish,
+            out_shape=(
+                jax.ShapeDtypeStruct((1, width, width), jnp.bfloat16),
+                jax.ShapeDtypeStruct((1, width), jnp.float32),
+            ),
+            in_specs=[vmem] * 4,
+            out_specs=(any_space, any_space),
+            scratch_shapes=[
+                pltpu.VMEM((width, width), jnp.bfloat16),
+                pltpu.SemaphoreType.DMA((width // STORE,)),
+                pltpu.SemaphoreType.DMA,
+            ],
+            compiler_params=pltpu.CompilerParams(vmem_limit_bytes=24 * 2**20),
+            cost_estimate=pl.CostEstimate(
+                flops=2 * TAIL * width * width,
+                bytes_accessed=6 * width * width,
+                transcendentals=0,
+            ),
+        )(*parts)
 
     spec = P("depth", None, None)
     return jax.shard_map(

time: 111 us -> 106 us (0.955)
  local copies, waits for them, and re-layouts: 3.68 us -> 0 us
  Pallas kernels: 107 us -> 105 us
    unnamed x4 -> x0, local copies, waits for them, and re-layouts: 3.68 us -> none
    pallas_call x1 -> x2, Pallas kernels: 107 us -> 105 us  [the longest x1 103 us: step(): pl.pallas_call(functools.partial(kernel, n), out_shape=(pltpu.VMEM((width...]
where the time goes in v2:
time: 106 us
  Pallas kernels  105 us (99%)
    pallas_call x1, Pallas kernels, step(): pl.pallas_call(functools.partial(kernel, n), out_shape=(pltpu.VMEM((width...  103 us

profile of v2, /device:TPU:24, one launch (start us, length us, event | category | flops | bytes accessed | tf_op | source)
XLA Modules:
  0.0 105.6 jit_solution(17717486182387473260)
XLA Ops:
  0.6 103.1 %shard_map.59 = (f32[1024,1024]{1,0:T(8,128)S(1)}, bf16[64,1024]{1,0:T(8,128)(2,1)S(1)}, bf16[64,1024]{1,0:T(8,128)(2,1)S(1)}, f32[1,1024]{1,0:T(1,128)S(1)}) custom-call(bf16[1,1024,1024]{2,1,0:T(8,128)(2,1)} %weights_ref.1, f32[1,1024]{1,0:T(1,128)} %gains_ref.1, f32[1,512,1024]{2,1,0:T(8,128)} %states_ref.1, f32[1,512,1024]{2,1,0:T(8,128)} %adjoints_ref.1), custom_call_target="tpu_custom_call" | custom-call | flops 11811160064 | bytes 8388608 | tf_op jit(solution)/shard_map/pallas_call | solution.py:290
  103.8 1.6 %shard_map.60 = (bf16[1,1024,1024]{2,1,0:T(8,128)(2,1)}, f32[1,1024]{1,0:T(1,128)}) custom-call(f32[1024,1024]{1,0:T(8,128)S(1)} %get-tuple-element.6.total, bf16[64,1024]{1,0:T(8,128)(2,1)S(1)} %get-tuple-element.7.scaled_tail, bf16[64,1024]{1,0:T(8,128)(2,1)S(1)} %get-tuple-element.8.pre_grad_tail, f32[1,1024]{1,0:T(1,128)S(1)} %get-tuple-element.9.gain_total), custom_call_target="tpu_custom_call" | custom-call | flops 134217728 | bytes 6291456 | tf_op jit(solution)/shard_map/pallas_call | solution.py:327

commit v3 on v2

--- a/solution.py
+++ b/solution.py
@@ -12,6 +12,14 @@
 MESH = pl.DeviceIdType.MESH
 CHUNKS = (64, 128, 128, 128, 64)
 TAIL = 64
+COLUMN = 16
+ROW = 4
+FIRST_RELAY = 9
+SECOND_RELAY = 3
+FIRST_AFTER = 1
+SECOND_AFTER = 2
+DETOUR = 32
+DETOUR_CHUNK = 3
 STORE = 128
 TILE = 256
 
@@ -42,6 +50,9 @@
     adjoint_sem,
     state_send_sem,
     adjoint_send_sem,
+    relay,
+    relay_sem,
+    relay_send_sem,
 ):
     me = lax.axis_index("depth")
     right, left = lax.rem(me + 1, n), lax.rem(me + n - 1, n)
@@ -51,9 +62,29 @@
     starts = [sum(CHUNKS[:c]) for c in range(len(CHUNKS))]
     chunks = list(enumerate(zip(starts, CHUNKS)))
 
+    column, place = me // COLUMN, lax.rem(me, COLUMN)
+    crosses = jnp.logical_and(lax.rem(column, ROW) == ROW - 1, column < n // COLUMN - 1)
+    crossed = jnp.logical_and(lax.rem(column, ROW) == 0, column > 0)
+    diverts = jnp.logical_and(crosses, place == COLUMN - 1)
+    relays_first = jnp.logical_and(crosses, place == FIRST_RELAY)
+    relays_second = jnp.logical_and(crossed, place == SECOND_RELAY)
+    ends = jnp.logical_and(crossed, place == 0)
+    first_relay = lax.rem(me + n - (COLUMN - 1 - FIRST_RELAY), n)
+    second_relay = lax.rem(me + COLUMN - (FIRST_RELAY - SECOND_RELAY), n)
+    end = lax.rem(me + n - SECOND_RELAY, n)
+
     barrier = pltpu.get_barrier_semaphore()
     for neighbour in (left, right):
         pl.semaphore_signal(barrier, inc=1, device_id=(neighbour,), device_id_type=MESH)
+    for receives, sender in (
+        (relays_first, lax.rem(me + COLUMN - 1 - FIRST_RELAY, n)),
+        (relays_second, lax.rem(me + n - COLUMN + FIRST_RELAY - SECOND_RELAY, n)),
+        (ends, lax.rem(me + SECOND_RELAY, n)),
+    ):
+
+        @pl.when(receives)
+        def _():
+            pl.semaphore_signal(barrier, inc=1, device_id=(sender,), device_id_type=MESH)
 
     def load_state(sweep, c):
         rows = pl.ds(starts[c], CHUNKS[c])
@@ -76,6 +107,62 @@
             send_sem=state_send_sem.at[slot, c],
             recv_sem=state_sem.at[sweep + 1, c],
             device_id=(right,),
+            device_id_type=MESH,
+        )
+
+    def send_state_tile(c, t):
+        rows = pl.ds(starts[c], CHUNKS[c])
+        columns = pl.ds(t * TILE, TILE)
+        return pltpu.make_async_remote_copy(
+            src_ref=state_out.at[0, rows, columns],
+            dst_ref=state.at[1, rows, columns],
+            send_sem=state_send_sem.at[0, c],
+            recv_sem=state_sem.at[1, c],
+            device_id=(right,),
+            device_id_type=MESH,
+        )
+
+    detour_start = starts[DETOUR_CHUNK] + CHUNKS[DETOUR_CHUNK] - DETOUR
+    detour = pl.ds(detour_start, DETOUR)
+
+    def send_direct():
+        rows = pl.ds(starts[DETOUR_CHUNK], CHUNKS[DETOUR_CHUNK] - DETOUR)
+        return pltpu.make_async_remote_copy(
+            src_ref=state_out.at[0, rows],
+            dst_ref=state.at[1, rows],
+            send_sem=state_send_sem.at[0, DETOUR_CHUNK],
+            recv_sem=state_sem.at[1, DETOUR_CHUNK],
+            device_id=(right,),
+            device_id_type=MESH,
+        )
+
+    def send_detour():
+        return pltpu.make_async_remote_copy(
+            src_ref=state_out.at[0, detour],
+            dst_ref=relay,
+            send_sem=state_send_sem.at[0, DETOUR_CHUNK],
+            recv_sem=relay_sem,
+            device_id=(first_relay,),
+            device_id_type=MESH,
+        )
+
+    def pass_on():
+        return pltpu.make_async_remote_copy(
+            src_ref=relay,
+            dst_ref=relay,
+            send_sem=relay_send_sem,
+            recv_sem=relay_sem,
+            device_id=(second_relay,),
+            device_id_type=MESH,
+        )
+
+    def deliver():
+        return pltpu.make_async_remote_copy(
+            src_ref=relay,
+            dst_ref=state.at[1, detour],
+            send_sem=relay_send_sem,
+            recv_sem=state_sem.at[1, DETOUR_CHUNK],
+            device_id=(end,),
             device_id_type=MESH,
         )
 
@@ -146,6 +233,14 @@
             slope[pl.ds(0, count), columns] = squash * (1.0 + preact * (1.0 - squash))
             if not last:
                 state_out[slot, rows, columns] = state[sweep, rows, columns] + preact * squash
+            if first and c == 0:
+                if t == 0:
+                    more = jnp.logical_or(diverts, jnp.logical_or(relays_first, relays_second))
+                    pl.semaphore_wait(barrier, jnp.where(more, 3, 2))
+
+                @pl.when(me < n - 1)
+                def _():
+                    send_state_tile(c, t).start()
         return inverse
 
     def backward(sweep, c, inverse, last):
@@ -189,12 +284,22 @@
                 send_adjoint(sweep - 2, c).wait_send()
 
         inverse = forward(sweep, c, first, False)
-        if first and c == 0:
-            pl.semaphore_wait(barrier, 2)
-
-        @pl.when(me < n - 1)
-        def _():
-            send_state(sweep, c).start()
+        if first and c == DETOUR_CHUNK:
+
+            @pl.when(diverts)
+            def _():
+                send_direct().start()
+                send_detour().start()
+
+            @pl.when(jnp.logical_and(me < n - 1, jnp.logical_not(diverts)))
+            def _():
+                send_state(sweep, c).start()
+
+        elif not (first and c == 0):
+
+            @pl.when(me < n - 1)
+            def _():
+                send_state(sweep, c).start()
 
         backward(sweep, c, inverse, False)
 
@@ -209,6 +314,20 @@
     def _(sweep):
         for c, _ in chunks:
             sweep_chunk(sweep, c, False)
+            if c == FIRST_AFTER:
+
+                @pl.when(jnp.logical_and(sweep == 1, relays_first))
+                def _():
+                    pass_on().wait_recv()
+                    pass_on().start()
+
+            if c == SECOND_AFTER:
+
+                @pl.when(jnp.logical_and(sweep == 1, relays_second))
+                def _():
+                    pass_on().wait_recv()
+                    deliver().start()
+
 
     for c, (start, count) in chunks:
         rows = pl.ds(start, count)
@@ -228,6 +347,14 @@
                     preferred_element_type=jnp.float32,
                 )
                 total[columns, :] = part if c == 0 else total[columns, :] + part
+
+    @pl.when(relays_first)
+    def _():
+        pass_on().wait_send()
+
+    @pl.when(relays_second)
+    def _():
+        deliver().wait_send()
 
     for sweep in range(SWEEPS - 2, SWEEPS):
         for c, _ in chunks:
@@ -314,6 +441,9 @@
                 pltpu.SemaphoreType.DMA((SWEEPS + 1, len(CHUNKS))),
                 pltpu.SemaphoreType.DMA((2, len(CHUNKS))),
                 pltpu.SemaphoreType.DMA((2, len(CHUNKS))),
+                pltpu.VMEM((DETOUR, width), jnp.float32),
+                pltpu.SemaphoreType.DMA,
+                pltpu.SemaphoreType.DMA,
             ],
             compiler_params=pltpu.CompilerParams(
                 collective_id=0, has_side_effects=True, vmem_limit_bytes=48 * 2**20

time: 106 us -> 104 us (0.981)
  Pallas kernels: 105 us -> 103 us
    pallas_call x1, Pallas kernels: 103 us -> 102 us  [step(): pl.pallas_call(functools.partial(kernel, n), out_shape=(pltpu.VMEM((width...]
where the time goes in v3:
time: 104 us
  Pallas kernels  103 us (99%)
    pallas_call x1, Pallas kernels, step(): pl.pallas_call(functools.partial(kernel, n), out_shape=(pltpu.VMEM((width...  102 us

profile of v3, /device:TPU:24, one launch (start us, length us, event | category | flops | bytes accessed | tf_op | source)
XLA Modules:
  0.0 104.0 jit_solution(12761165347453978709)
XLA Ops:
  0.6 101.6 %shard_map.59 = (f32[1024,1024]{1,0:T(8,128)S(1)}, bf16[64,1024]{1,0:T(8,128)(2,1)S(1)}, bf16[64,1024]{1,0:T(8,128)(2,1)S(1)}, f32[1,1024]{1,0:T(1,128)S(1)}) custom-call(bf16[1,1024,1024]{2,1,0:T(8,128)(2,1)} %weights_ref.1, f32[1,1024]{1,0:T(1,128)} %gains_ref.1, f32[1,512,1024]{2,1,0:T(8,128)} %states_ref.1, f32[1,512,1024]{2,1,0:T(8,128)} %adjoints_ref.1), custom_call_target="tpu_custom_call" | custom-call | flops 11811160064 | bytes 8388608 | tf_op jit(solution)/shard_map/pallas_call | solution.py:417
  102.2 1.7 %shard_map.60 = (bf16[1,1024,1024]{2,1,0:T(8,128)(2,1)}, f32[1,1024]{1,0:T(1,128)}) custom-call(f32[1024,1024]{1,0:T(8,128)S(1)} %get-tuple-element.6.total, bf16[64,1024]{1,0:T(8,128)(2,1)S(1)} %get-tuple-element.7.scaled_tail, bf16[64,1024]{1,0:T(8,128)(2,1)S(1)} %get-tuple-element.8.pre_grad_tail, f32[1,1024]{1,0:T(1,128)S(1)} %get-tuple-element.9.gain_total), custom_call_target="tpu_custom_call" | custom-call | flops 134217728 | bytes 6291456 | tf_op jit(solution)/shard_map/pallas_call | solution.py:457

commit v4 on v3

--- a/solution.py
+++ b/solution.py
@@ -10,16 +10,16 @@
 SWEEPS = 4
 EPS = 1e-06
 MESH = pl.DeviceIdType.MESH
-CHUNKS = (64, 128, 128, 128, 64)
+CHUNKS = (64, 192, 192, 64)
 TAIL = 64
 COLUMN = 16
 ROW = 4
 FIRST_RELAY = 9
 SECOND_RELAY = 3
 FIRST_AFTER = 1
-SECOND_AFTER = 2
+SECOND_AFTER = 1
 DETOUR = 32
-DETOUR_CHUNK = 3
+DETOUR_CHUNK = 2
 STORE = 128
 TILE = 256
 

time: 104 us -> 104 us (level)
  no operation moved by 1% of the time
where the time goes in v4:
time: 104 us
  Pallas kernels  103 us (99%)
    pallas_call x1, Pallas kernels, step(): pl.pallas_call(functools.partial(kernel, n), out_shape=(pltpu.VMEM((width...  101 us

profile of v4, /device:TPU:24, one launch (start us, length us, event | category | flops | bytes accessed | tf_op | source)
XLA Modules:
  0.0 103.9 jit_solution(9698571617651900628)
XLA Ops:
  0.6 101.4 %shard_map.59 = (f32[1024,1024]{1,0:T(8,128)S(1)}, bf16[64,1024]{1,0:T(8,128)(2,1)S(1)}, bf16[64,1024]{1,0:T(8,128)(2,1)S(1)}, f32[1,1024]{1,0:T(1,128)S(1)}) custom-call(bf16[1,1024,1024]{2,1,0:T(8,128)(2,1)} %weights_ref.1, f32[1,1024]{1,0:T(1,128)} %gains_ref.1, f32[1,512,1024]{2,1,0:T(8,128)} %states_ref.1, f32[1,512,1024]{2,1,0:T(8,128)} %adjoints_ref.1), custom_call_target="tpu_custom_call" | custom-call | flops 11811160064 | bytes 8388608 | tf_op jit(solution)/shard_map/pallas_call | solution.py:417
  102.1 1.6 %shard_map.60 = (bf16[1,1024,1024]{2,1,0:T(8,128)(2,1)}, f32[1,1024]{1,0:T(1,128)}) custom-call(f32[1024,1024]{1,0:T(8,128)S(1)} %get-tuple-element.6.total, bf16[64,1024]{1,0:T(8,128)(2,1)S(1)} %get-tuple-element.7.scaled_tail, bf16[64,1024]{1,0:T(8,128)(2,1)S(1)} %get-tuple-element.8.pre_grad_tail, f32[1,1024]{1,0:T(1,128)S(1)} %get-tuple-element.9.gain_total), custom_call_target="tpu_custom_call" | custom-call | flops 134217728 | bytes 6291456 | tf_op jit(solution)/shard_map/pallas_call | solution.py:457
